TPU v7x, 32 devices: a whole 2x2x4 slice. The times are simulated.
32 devices in a mesh: section: 8 (over z, core), tensor: 4 (over y, x).
Axes of the slice: x: 2, y: 2, z: 4, core: 2. Of those that a mesh axis runs over, the one named last changes fastest.
Arguments:
- section_inputs: bfloat16 [8, 2, 8192, 128], P('section', None, 'tensor'), may hold values from -6 to 6
- arriving_grad: bfloat16 [8, 8192, 128], P('section', 'tensor'), may hold values from -1.5 to 1.5
- loss_grad: bfloat16 [1, 8192, 128], P(None, 'tensor'), may hold values from -1.5 to 1.5
- factor_first: bfloat16 [8, 3, 64, 128, 128], P('section', None, 'tensor'), may hold values from -0.5 to 0.5
- factor_second: bfloat16 [8, 3, 64, 128, 128], P('section', None, 'tensor'), may hold values from -0.5 to 0.5
- gate_scales: float32 [8, 3, 8192], P('section', None, 'tensor'), may hold values from 0.25 to 1.5
- layer_count: int32 [8], P('section'), may hold values from 1 to 3, as said below
Outputs:
- last_emitted: bfloat16 [8, 8192, 128], P('section', 'tensor')
- factor_first_grad: bfloat16 [8, 3, 64, 128, 128], P('section', None, 'tensor')
- factor_second_grad: bfloat16 [8, 3, 64, 128, 128], P('section', None, 'tensor')
- gate_grad: float32 [8, 3, 8192], P('section', None, 'tensor')
Inputs may be any that keep to these rules, and one draw needn't show every extreme that they name: `layer_count`: every section runs at least one layer and some section runs 3.
All inputs are finite; a program needn't handle non-finite values.
Results may differ from a plain program's by a relative error of at most 0.017.
Values may be sent and summed in bfloat16 or wider, within the bound.
A program may use at most 64 MiB of HBM per device.

v0:
```python
import jax
import jax.numpy as jnp
from jax import lax
from jax.sharding import PartitionSpec as P


def from_behind(value, axis, steps):
    count = lax.axis_size(axis)
    initial, last = (max(0, -steps), min(count, count - steps))
    return lax.ppermute(value, axis, [(source, source + steps) for source in range(initial, last)])


def permute_blocks(values):
    tensor_size = lax.axis_size("tensor")
    batch_count, local_blocks, block_size, token_count = values.shape
    blocks_all = local_blocks * tensor_size
    repeat_count = block_size // blocks_all
    shaped = values.reshape(
        batch_count, local_blocks, tensor_size, local_blocks, repeat_count, token_count
    )
    moved = lax.all_to_all(shaped, "tensor", split_axis=2, concat_axis=1, tiled=True)
    moved = moved.reshape(batch_count, blocks_all, local_blocks, repeat_count, token_count)
    return moved.transpose(0, 2, 3, 1, 4).reshape(
        batch_count, local_blocks, block_size, token_count
    )


def unpermute_blocks(values):
    tensor_size = lax.axis_size("tensor")
    local_blocks, block_size, token_count = values.shape
    blocks_all = local_blocks * tensor_size
    repeat_count = block_size // blocks_all
    shaped = values.reshape(local_blocks, repeat_count, tensor_size, local_blocks, token_count)
    moved = lax.all_to_all(shaped, "tensor", split_axis=2, concat_axis=0, tiled=True)
    moved = moved.reshape(blocks_all, repeat_count, local_blocks, token_count)
    return moved.transpose(2, 0, 1, 3).reshape(local_blocks, block_size, token_count)


def recompute(initial, factor_one, factor_two, gate_rows, layer_total):
    slot_count = factor_one.shape[0]
    hidden = initial
    saved = []
    for layer_slot in range(slot_count):
        first_out = jnp.einsum(
            "kij,mkjt->mkit", factor_one[layer_slot], hidden, preferred_element_type=jnp.float32
        ).astype(jnp.bfloat16)
        permuted = permute_blocks(first_out)
        mixed = jnp.einsum(
            "kij,mkjt->mkit", factor_two[layer_slot], permuted, preferred_element_type=jnp.float32
        )
        gate_now = gate_rows[layer_slot][None, :, :, None]
        next_hidden = (
            hidden.astype(jnp.float32) + gate_now * (mixed * jax.nn.sigmoid(mixed))
        ).astype(jnp.bfloat16)
        saved.append((hidden, permuted, mixed))
        hidden = jnp.where(layer_slot < layer_total, next_hidden, hidden)
    return saved


def shards(
    section_inputs, arriving_grad, loss_grad, factor_first, factor_second, gate_scales, layer_count
):
    moments = section_inputs.shape[1]
    slot_count = factor_first.shape[1]
    local_blocks = factor_first.shape[2]
    block_size = factor_first.shape[3]
    token_count = section_inputs.shape[3]
    first_local = factor_first[0]
    second_local = factor_second[0]
    gate_rows = gate_scales[0].reshape(slot_count, local_blocks, block_size)
    layer_total = layer_count[0]
    section_id = lax.axis_index("section")
    last_section = lax.axis_size("section") - 1
    inputs_local = section_inputs[0].reshape(moments, local_blocks, block_size, token_count)
    first_acc = [
        jnp.zeros((local_blocks, block_size, block_size), jnp.float32) for slot in range(slot_count)
    ]
    second_acc = [
        jnp.zeros((local_blocks, block_size, block_size), jnp.float32) for slot in range(slot_count)
    ]
    gate_acc = [jnp.zeros((local_blocks, block_size), jnp.float32) for slot in range(slot_count)]
    emitted = None
    for moment in range(moments):
        if moment == 0:
            arrived = arriving_grad[0].reshape(local_blocks, block_size, token_count)
        else:
            shifted = from_behind(emitted, "section", -1)
            from_loss = loss_grad[moment - 1].reshape(local_blocks, block_size, token_count)
            arrived = jnp.where(section_id == last_section, from_loss, shifted)
        computed = recompute(
            inputs_local[moment : moment + 1], first_local, second_local, gate_rows, layer_total
        )
        saved = [(record[0][0], record[1][0], record[2][0]) for record in computed]
        grad_now = arrived.astype(jnp.float32)
        for layer_slot in reversed(range(slot_count)):
            hidden, permuted, mixed = saved[layer_slot]
            is_live = layer_slot < layer_total
            logistic = jax.nn.sigmoid(mixed)
            gate_now = gate_rows[layer_slot][:, :, None]
            gate_term = jnp.sum(grad_now * (mixed * logistic), axis=2)
            gate_acc[layer_slot] = gate_acc[layer_slot] + jnp.where(
                is_live, gate_term, jnp.zeros_like(gate_term)
            )
            scaled = (grad_now * gate_now * logistic * (1.0 + mixed * (1.0 - logistic))).astype(
                jnp.bfloat16
            )
            backed = jnp.einsum(
                "kji,kjt->kit", second_local[layer_slot], scaled, preferred_element_type=jnp.float32
            ).astype(jnp.bfloat16)
            returned = unpermute_blocks(backed)
            moved_grad = grad_now + jnp.einsum(
                "kji,kjt->kit",
                first_local[layer_slot],
                returned,
                preferred_element_type=jnp.float32,
            )
            grad_now = jnp.where(is_live, moved_grad, grad_now)
            second_term = jnp.einsum(
                "kit,kjt->kij", scaled, permuted, preferred_element_type=jnp.float32
            )
            first_term = jnp.einsum(
                "kit,kjt->kij", returned, hidden, preferred_element_type=jnp.float32
            )
            second_acc[layer_slot] = second_acc[layer_slot] + jnp.where(
                is_live, second_term, jnp.zeros_like(second_term)
            )
            first_acc[layer_slot] = first_acc[layer_slot] + jnp.where(
                is_live, first_term, jnp.zeros_like(first_term)
            )
        emitted = grad_now.astype(jnp.bfloat16)
    last_emitted = emitted.reshape(1, local_blocks * block_size, token_count)
    gate_out = jnp.stack(gate_acc).reshape(1, slot_count, local_blocks * block_size)
    first_out = jnp.stack(first_acc).astype(jnp.bfloat16)[None]
    second_out = jnp.stack(second_acc).astype(jnp.bfloat16)[None]
    return (last_emitted, first_out, second_out, gate_out)


def solution(mesh):
    in_specs = (
        P("section", None, "tensor", None),
        P("section", "tensor", None),
        P(None, "tensor", None),
        P("section", None, "tensor", None, None),
        P("section", None, "tensor", None, None),
        P("section", None, "tensor"),
        P("section"),
    )
    out_specs = (
        P("section", "tensor", None),
        P("section", None, "tensor", None, None),
        P("section", None, "tensor", None, None),
        P("section", None, "tensor"),
    )
    return jax.shard_map(shards, mesh=mesh, in_specs=in_specs, out_specs=out_specs, check_vma=False)
```

profile of v0, /device:TPU:0, one launch (start us, length us, event | category | flops | bytes accessed | tf_op | source)
XLA Modules:
  0.0 212.1 jit_solution(17580493403781569105)
XLA Ops:
  3.5 5.2 %all-to-all-start.6 = ((bf16[1,16,4,16,2,128]{5,3,4,1,0,2:T(8,128)(2,1)}), bf16[1,16,4,16,2,128]{5,3,4,1,0,2:T(8,128)(2,1)}, u32[]{:S(2)}, u32[]{:S(2)}) async-start(bf16[1,16,4,16,2,128]{5,3,4,1,0,2:T(8,128)(2,1)} %copy.185), calls=%async_computation.6 | async-start | bytes 1048576 | tf_op jit(solution)/shard_map/all_to_all | solution.py:21
  12.6 4.7 %all-to-all-done.6 = bf16[1,16,4,16,2,128]{5,3,4,1,0,2:T(8,128)(2,1)} async-done(((bf16[1,16,4,16,2,128]{5,3,4,1,0,2:T(8,128)(2,1)}), bf16[1,16,4,16,2,128]{5,3,4,1,0,2:T(8,128)(2,1)}, u32[]{:S(2)}, u32[]{:S(2)}) %all-to-all-start.6) | async-done | bytes 524320 | tf_op jit(solution)/shard_map/all_to_all | solution.py:21
  17.2 4.1 %all-to-all-start = ((bf16[1,16,4,16,2,128]{5,3,4,1,0,2:T(8,128)(2,1)}), bf16[1,16,4,16,2,128]{5,3,4,1,0,2:T(8,128)(2,1)}, u32[]{:S(2)}, u32[]{:S(2)}) async-start(bf16[1,16,4,16,2,128]{5,3,4,1,0,2:T(8,128)(2,1)} %copy.157), calls=%async_computation | async-start | bytes 1048576 | tf_op jit(solution)/shard_map/all_to_all | solution.py:21
  23.4 5.6 %all-to-all-done = bf16[1,16,4,16,2,128]{5,3,4,1,0,2:T(8,128)(2,1)} async-done(((bf16[1,16,4,16,2,128]{5,3,4,1,0,2:T(8,128)(2,1)}), bf16[1,16,4,16,2,128]{5,3,4,1,0,2:T(8,128)(2,1)}, u32[]{:S(2)}, u32[]{:S(2)}) %all-to-all-start) | async-done | bytes 524320 | tf_op jit(solution)/shard_map/all_to_all | solution.py:21
  36.2 4.1 %all-to-all-start.1 = ((bf16[1,16,4,16,2,128]{5,3,4,1,0,2:T(8,128)(2,1)}), bf16[1,16,4,16,2,128]{5,3,4,1,0,2:T(8,128)(2,1)}, u32[]{:S(2)}, u32[]{:S(2)}) async-start(bf16[1,16,4,16,2,128]{5,3,4,1,0,2:T(8,128)(2,1)} %copy.162), calls=%async_computation.1 | async-start | bytes 1048576 | tf_op jit(solution)/shard_map/all_to_all | solution.py:21
  42.8 4.4 %all-to-all-done.1 = bf16[1,16,4,16,2,128]{5,3,4,1,0,2:T(8,128)(2,1)} async-done(((bf16[1,16,4,16,2,128]{5,3,4,1,0,2:T(8,128)(2,1)}), bf16[1,16,4,16,2,128]{5,3,4,1,0,2:T(8,128)(2,1)}, u32[]{:S(2)}, u32[]{:S(2)}) %all-to-all-start.1) | async-done | bytes 524320 | tf_op jit(solution)/shard_map/all_to_all | solution.py:21
  47.2 4.1 %all-to-all-start.7 = ((bf16[1,16,4,16,2,128]{5,3,4,1,0,2:T(8,128)(2,1)}), bf16[1,16,4,16,2,128]{5,3,4,1,0,2:T(8,128)(2,1)}, u32[]{:S(2)}, u32[]{:S(2)}) async-start(bf16[1,16,4,16,2,128]{5,3,4,1,0,2:T(8,128)(2,1)} %copy.190), calls=%async_computation.7 | async-start | bytes 1048576 | tf_op jit(solution)/shard_map/all_to_all | solution.py:21
  53.4 4.6 %all-to-all-done.7 = bf16[1,16,4,16,2,128]{5,3,4,1,0,2:T(8,128)(2,1)} async-done(((bf16[1,16,4,16,2,128]{5,3,4,1,0,2:T(8,128)(2,1)}), bf16[1,16,4,16,2,128]{5,3,4,1,0,2:T(8,128)(2,1)}, u32[]{:S(2)}, u32[]{:S(2)}) %all-to-all-start.7) | async-done | bytes 524320 | tf_op jit(solution)/shard_map/all_to_all | solution.py:21
  64.9 4.1 %all-to-all-start.2 = ((bf16[1,16,4,16,2,128]{5,3,4,1,0,2:T(8,128)(2,1)}), bf16[1,16,4,16,2,128]{5,3,4,1,0,2:T(8,128)(2,1)}, u32[]{:S(2)}, u32[]{:S(2)}) async-start(bf16[1,16,4,16,2,128]{5,3,4,1,0,2:T(8,128)(2,1)} %copy.166), calls=%async_computation.2 | async-start | bytes 1048576 | tf_op jit(solution)/shard_map/all_to_all | solution.py:21
  71.2 4.4 %all-to-all-done.2 = bf16[1,16,4,16,2,128]{5,3,4,1,0,2:T(8,128)(2,1)} async-done(((bf16[1,16,4,16,2,128]{5,3,4,1,0,2:T(8,128)(2,1)}), bf16[1,16,4,16,2,128]{5,3,4,1,0,2:T(8,128)(2,1)}, u32[]{:S(2)}, u32[]{:S(2)}) %all-to-all-start.2) | async-done | bytes 524320 | tf_op jit(solution)/shard_map/all_to_all | solution.py:21
  76.9 3.0 %fusion.75 = (bf16[16,128,128]{1,2,0:T(8,128)(2,1)S(1)}, f32[16,128,128]{2,1,0:T(8,128)}) fusion(f32[16,128,128]{1,2,0:T(8,128)} %copy.173, f32[16,128]{1,0:T(8,128)S(1)} %bitcast.599, bf16[16,128,128]{2,1,0:T(8,128)(2,1)S(1)} %bitcast.594, bf16[1,3,16,128,128]{4,3,2,1,0:T(8,128)(2,1)S(1)} %copy-done), kind=kOutput, calls=%fused_computation.137 | convolution fusion | flops 69730304 | bytes 3678208 | tf_op jit(solution)/shard_map/kij,mkjt->mkit/dot_general | solution.py:48
  82.1 4.1 %all-to-all-start.3 = ((bf16[16,2,4,16,128]{4,3,1,0,2:T(8,128)(2,1)}), bf16[16,2,4,16,128]{4,3,1,0,2:T(8,128)(2,1)}, u32[]{:S(2)}, u32[]{:S(2)}) async-start(bf16[16,2,4,16,128]{4,3,1,0,2:T(8,128)(2,1)} %copy.171), calls=%async_computation.3 | async-start | bytes 1048576 | tf_op jit(solution)/shard_map/all_to_all | solution.py:34
  86.2 6.6 %all-to-all-done.3 = bf16[16,2,4,16,128]{4,3,1,0,2:T(8,128)(2,1)} async-done(((bf16[16,2,4,16,128]{4,3,1,0,2:T(8,128)(2,1)}), bf16[16,2,4,16,128]{4,3,1,0,2:T(8,128)(2,1)}, u32[]{:S(2)}, u32[]{:S(2)}) %all-to-all-start.3) | async-done | bytes 524320 | tf_op jit(solution)/shard_map/all_to_all | solution.py:34
  95.9 9.7 %all_to_all.180 = bf16[16,2,4,16,128]{4,3,1,0,2:T(8,128)(2,1)S(1)} all-to-all(bf16[16,2,4,16,128]{4,3,1,0,2:T(8,128)(2,1)S(1)} %copy.177), channel_id=1, replica_groups=mesh['section'=8,'tensor'=4] {'tensor'}, dimensions={2} | all-to-all | bytes 1048576 | tf_op jit(solution)/shard_map/all_to_all | solution.py:34
  109.5 4.1 %all-to-all-start.5 = ((bf16[16,2,4,16,128]{4,3,1,0,2:T(8,128)(2,1)}), bf16[16,2,4,16,128]{4,3,1,0,2:T(8,128)(2,1)}, u32[]{:S(2)}, u32[]{:S(2)}) async-start(bf16[16,2,4,16,128]{4,3,1,0,2:T(8,128)(2,1)} %copy.181), calls=%async_computation.5 | async-start | bytes 1048576 | tf_op jit(solution)/shard_map/all_to_all | solution.py:34
  116.1 5.5 %all-to-all-done.5 = bf16[16,2,4,16,128]{4,3,1,0,2:T(8,128)(2,1)} async-done(((bf16[16,2,4,16,128]{4,3,1,0,2:T(8,128)(2,1)}), bf16[16,2,4,16,128]{4,3,1,0,2:T(8,128)(2,1)}, u32[]{:S(2)}, u32[]{:S(2)}) %all-to-all-start.5) | async-done | bytes 524320 | tf_op jit(solution)/shard_map/all_to_all | solution.py:34
  121.6 4.1 %all-to-all-start.8 = ((bf16[1,16,4,16,2,128]{5,3,4,1,0,2:T(8,128)(2,1)}), bf16[1,16,4,16,2,128]{5,3,4,1,0,2:T(8,128)(2,1)}, u32[]{:S(2)}, u32[]{:S(2)}) async-start(bf16[1,16,4,16,2,128]{5,3,4,1,0,2:T(8,128)(2,1)} %copy.194), calls=%async_computation.8 | async-start | bytes 1048576 | tf_op jit(solution)/shard_map/all_to_all | solution.py:21
  143.2 4.1 %all-to-all-start.9 = ((bf16[16,2,4,16,128]{4,3,1,0,2:T(8,128)(2,1)}), bf16[16,2,4,16,128]{4,3,1,0,2:T(8,128)(2,1)}, u32[]{:S(2)}, u32[]{:S(2)}) async-start(bf16[16,2,4,16,128]{4,3,1,0,2:T(8,128)(2,1)} %copy.199), calls=%async_computation.9 | async-start | bytes 1048576 | tf_op jit(solution)/shard_map/all_to_all | solution.py:34
  150.1 6.6 %all-to-all-done.9 = bf16[16,2,4,16,128]{4,3,1,0,2:T(8,128)(2,1)} async-done(((bf16[16,2,4,16,128]{4,3,1,0,2:T(8,128)(2,1)}), bf16[16,2,4,16,128]{4,3,1,0,2:T(8,128)(2,1)}, u32[]{:S(2)}, u32[]{:S(2)}) %all-to-all-start.9) | async-done | bytes 524320 | tf_op jit(solution)/shard_map/all_to_all | solution.py:34
  158.2 3.2 %fusion.43 = (f32[16,128]{1,0:T(8,128)S(1)}, bf16[16,128,128]{1,2,0:T(8,128)(2,1)S(1)}, f32[16,128,128]{1,2,0:T(8,128)}) fusion(f32[16,128,128]{2,1,0:T(8,128)} %copy-done.35, f32[16,128]{1,0:T(8,128)S(1)} %bitcast.610, bf16[16,128,128]{2,1,0:T(8,128)(2,1)S(1)} %bitcast.575, bf16[1,3,16,128,128]{4,3,2,1,0:T(8,128)(2,1)S(1)} %copy-done.1, ...), kind=kOutput, calls=%fused_computation.93 | convolution fusion | flops 71301120 | bytes 4210689 | tf_op jit(solution)/shard_map/kji,kjt->kit/dot_general | solution.py:111
  167.5 4.1 %all-to-all-start.10 = ((bf16[16,2,4,16,128]{4,3,1,0,2:T(8,128)(2,1)}), bf16[16,2,4,16,128]{4,3,1,0,2:T(8,128)(2,1)}, u32[]{:S(2)}, u32[]{:S(2)}) async-start(bf16[16,2,4,16,128]{4,3,1,0,2:T(8,128)(2,1)} %copy.205), calls=%async_computation.10 | async-start | bytes 1048576 | tf_op jit(solution)/shard_map/all_to_all | solution.py:34
  174.3 5.8 %all-to-all-done.10 = bf16[16,2,4,16,128]{4,3,1,0,2:T(8,128)(2,1)} async-done(((bf16[16,2,4,16,128]{4,3,1,0,2:T(8,128)(2,1)}), bf16[16,2,4,16,128]{4,3,1,0,2:T(8,128)(2,1)}, u32[]{:S(2)}, u32[]{:S(2)}) %all-to-all-start.10) | async-done | bytes 524320 | tf_op jit(solution)/shard_map/all_to_all | solution.py:34
  192.7 4.3 %all-to-all-start.11 = ((bf16[16,2,4,16,128]{4,3,1,0,2:T(8,128)(2,1)}), bf16[16,2,4,16,128]{4,3,1,0,2:T(8,128)(2,1)}, u32[]{:S(2)}, u32[]{:S(2)}) async-start(bf16[16,2,4,16,128]{4,3,1,0,2:T(8,128)(2,1)} %copy.211), calls=%async_computation.11 | async-start | bytes 1048576 | tf_op jit(solution)/shard_map/all_to_all | solution.py:34
  200.3 4.2 %all-to-all-done.11 = bf16[16,2,4,16,128]{4,3,1,0,2:T(8,128)(2,1)} async-done(((bf16[16,2,4,16,128]{4,3,1,0,2:T(8,128)(2,1)}), bf16[16,2,4,16,128]{4,3,1,0,2:T(8,128)(2,1)}, u32[]{:S(2)}, u32[]{:S(2)}) %all-to-all-start.11) | async-done | bytes 524320 | tf_op jit(solution)/shard_map/all_to_all | solution.py:34
  (166 shorter events, 95.0 us)
Async XLA Ops:
  2.0 7.3 %copy-start.2 = (bf16[1,1,2048,128]{3,2,1,0:T(8,128)(2,1)}, bf16[1,1,2048,128]{3,2,1,0:T(8,128)(2,1)S(1)}, u32[]{:S(2)}) copy-start(bf16[1,1,2048,128]{3,2,1,0:T(8,128)(2,1)S(1)} %get-tuple-element.27) | copy-start | bytes 1572868
  2.0 9.3 %copy-start.4 = (bf16[1,1,2048,128]{3,2,1,0:T(8,128)(2,1)}, bf16[1,1,2048,128]{3,2,1,0:T(8,128)(2,1)S(1)}, u32[]{:S(2)}) copy-start(bf16[1,1,2048,128]{3,2,1,0:T(8,128)(2,1)S(1)} %get-tuple-element.26) | copy-start | bytes 1572868
  3.5 13.7 %all-to-all-start.6 = ((bf16[1,16,4,16,2,128]{5,3,4,1,0,2:T(8,128)(2,1)}), bf16[1,16,4,16,2,128]{5,3,4,1,0,2:T(8,128)(2,1)}, u32[]{:S(2)}, u32[]{:S(2)}) async-start(bf16[1,16,4,16,2,128]{5,3,4,1,0,2:T(8,128)(2,1)} %copy.185), calls=%async_computation.6 | async-start | bytes 1048576 | tf_op jit(solution)/shard_map/all_to_all | solution.py:21
  11.4 10.0 %copy-start.41 = (f32[1,3,2048]{2,0,1:T(1,128)S(1)}, f32[1,3,2048]{2,0,1:T(1,128)}, u32[]{:S(2)}) copy-start(f32[1,3,2048]{2,0,1:T(1,128)} %param.12) | copy-start | bytes 73732
  12.6 17.8 %copy-start = (bf16[1,3,16,128,128]{4,3,2,1,0:T(8,128)(2,1)S(1)}, bf16[1,3,16,128,128]{4,3,2,1,0:T(8,128)(2,1)}, u32[]{:S(2)}) copy-start(bf16[1,3,16,128,128]{4,3,2,1,0:T(8,128)(2,1)} %param.11) | copy-start | bytes 4718596
  17.2 11.8 %all-to-all-start = ((bf16[1,16,4,16,2,128]{5,3,4,1,0,2:T(8,128)(2,1)}), bf16[1,16,4,16,2,128]{5,3,4,1,0,2:T(8,128)(2,1)}, u32[]{:S(2)}, u32[]{:S(2)}) async-start(bf16[1,16,4,16,2,128]{5,3,4,1,0,2:T(8,128)(2,1)} %copy.157), calls=%async_computation | async-start | bytes 1048576 | tf_op jit(solution)/shard_map/all_to_all | solution.py:21
  30.4 3.6 %copy-start.23 = (bf16[1,16,2,64,128]{4,3,2,1,0:T(8,128)(2,1)}, bf16[1,16,2,64,128]{4,3,2,1,0:T(8,128)(2,1)S(1)}, u32[]{:S(2)}) copy-start(bf16[1,16,2,64,128]{4,3,2,1,0:T(8,128)(2,1)S(1)} %copy.158) | copy-start | bytes 1572868
  36.2 11.0 %all-to-all-start.1 = ((bf16[1,16,4,16,2,128]{5,3,4,1,0,2:T(8,128)(2,1)}), bf16[1,16,4,16,2,128]{5,3,4,1,0,2:T(8,128)(2,1)}, u32[]{:S(2)}, u32[]{:S(2)}) async-start(bf16[1,16,4,16,2,128]{5,3,4,1,0,2:T(8,128)(2,1)} %copy.162), calls=%async_computation.1 | async-start | bytes 1048576 | tf_op jit(solution)/shard_map/all_to_all | solution.py:21
  47.2 10.8 %all-to-all-start.7 = ((bf16[1,16,4,16,2,128]{5,3,4,1,0,2:T(8,128)(2,1)}), bf16[1,16,4,16,2,128]{5,3,4,1,0,2:T(8,128)(2,1)}, u32[]{:S(2)}, u32[]{:S(2)}) async-start(bf16[1,16,4,16,2,128]{5,3,4,1,0,2:T(8,128)(2,1)} %copy.190), calls=%async_computation.7 | async-start | bytes 1048576 | tf_op jit(solution)/shard_map/all_to_all | solution.py:21
  64.9 10.8 %all-to-all-start.2 = ((bf16[1,16,4,16,2,128]{5,3,4,1,0,2:T(8,128)(2,1)}), bf16[1,16,4,16,2,128]{5,3,4,1,0,2:T(8,128)(2,1)}, u32[]{:S(2)}, u32[]{:S(2)}) async-start(bf16[1,16,4,16,2,128]{5,3,4,1,0,2:T(8,128)(2,1)} %copy.166), calls=%async_computation.2 | async-start | bytes 1048576 | tf_op jit(solution)/shard_map/all_to_all | solution.py:21
  82.1 10.8 %all-to-all-start.3 = ((bf16[16,2,4,16,128]{4,3,1,0,2:T(8,128)(2,1)}), bf16[16,2,4,16,128]{4,3,1,0,2:T(8,128)(2,1)}, u32[]{:S(2)}, u32[]{:S(2)}) async-start(bf16[16,2,4,16,128]{4,3,1,0,2:T(8,128)(2,1)} %copy.171), calls=%async_computation.3 | async-start | bytes 1048576 | tf_op jit(solution)/shard_map/all_to_all | solution.py:34
  95.3 10.3 %copy-start.20 = (bf16[16,128,128]{1,2,0:T(8,128)(2,1)}, bf16[16,128,128]{1,2,0:T(8,128)(2,1)S(1)}, u32[]{:S(2)}) copy-start(bf16[16,128,128]{1,2,0:T(8,128)(2,1)S(1)} %get-tuple-element.23) | copy-start | bytes 1572868
  95.3 10.3 %copy-start.43 = (f32[16,128,128]{2,1,0:T(8,128)S(1)}, f32[16,128,128]{2,1,0:T(8,128)}, u32[]{:S(2)}) copy-start(f32[16,128,128]{2,1,0:T(8,128)} %get-tuple-element.35) | copy-start | bytes 3145732
  109.5 12.1 %all-to-all-start.5 = ((bf16[16,2,4,16,128]{4,3,1,0,2:T(8,128)(2,1)}), bf16[16,2,4,16,128]{4,3,1,0,2:T(8,128)(2,1)}, u32[]{:S(2)}, u32[]{:S(2)}) async-start(bf16[16,2,4,16,128]{4,3,1,0,2:T(8,128)(2,1)} %copy.181), calls=%async_computation.5 | async-start | bytes 1048576 | tf_op jit(solution)/shard_map/all_to_all | solution.py:34
  121.6 10.8 %all-to-all-start.8 = ((bf16[1,16,4,16,2,128]{5,3,4,1,0,2:T(8,128)(2,1)}), bf16[1,16,4,16,2,128]{5,3,4,1,0,2:T(8,128)(2,1)}, u32[]{:S(2)}, u32[]{:S(2)}) async-start(bf16[1,16,4,16,2,128]{5,3,4,1,0,2:T(8,128)(2,1)} %copy.194), calls=%async_computation.8 | async-start | bytes 1048576 | tf_op jit(solution)/shard_map/all_to_all | solution.py:21
  128.3 10.5 %collective-permute-start = (bf16[16,128,128]{1,2,0:T(8,128)(2,1)}, bf16[16,128,128]{1,2,0:T(8,128)(2,1)}, u32[]{:S(2)}, u32[]{:S(2)}) collective-permute-start(bf16[16,128,128]{1,2,0:T(8,128)(2,1)} %fusion.12), channel_id=1, source_target_pairs={{4,0},{8,4},{12,8},{16,12},{20,16},{24,20},{28,24},{5,1},{9,5},{13... | collective-permute-start | bytes 1572872 | tf_op jit(solution)/shard_map/ppermute | solution.py:10
  143.2 13.5 %all-to-all-start.9 = ((bf16[16,2,4,16,128]{4,3,1,0,2:T(8,128)(2,1)}), bf16[16,2,4,16,128]{4,3,1,0,2:T(8,128)(2,1)}, u32[]{:S(2)}, u32[]{:S(2)}) async-start(bf16[16,2,4,16,128]{4,3,1,0,2:T(8,128)(2,1)} %copy.199), calls=%async_computation.9 | async-start | bytes 1048576 | tf_op jit(solution)/shard_map/all_to_all | solution.py:34
  158.2 3.2 %copy-start.12 = (bf16[1,16,128,128]{2,3,1,0:T(8,128)(2,1)S(1)}, bf16[1,16,128,128]{2,3,1,0:T(8,128)(2,1)}, u32[]{:S(2)}) copy-start(bf16[1,16,128,128]{2,3,1,0:T(8,128)(2,1)} %get-tuple-element.32) | copy-start | bytes 1572868
  167.5 12.6 %all-to-all-start.10 = ((bf16[16,2,4,16,128]{4,3,1,0,2:T(8,128)(2,1)}), bf16[16,2,4,16,128]{4,3,1,0,2:T(8,128)(2,1)}, u32[]{:S(2)}, u32[]{:S(2)}) async-start(bf16[16,2,4,16,128]{4,3,1,0,2:T(8,128)(2,1)} %copy.205), calls=%async_computation.10 | async-start | bytes 1048576 | tf_op jit(solution)/shard_map/all_to_all | solution.py:34
  180.1 4.3 %copy-start.34 = (f32[16,128,128]{2,1,0:T(8,128)S(1)}, f32[16,128,128]{2,1,0:T(8,128)}, u32[]{:S(2)}) copy-start(f32[16,128,128]{2,1,0:T(8,128)} %copy-done.33) | copy-start | bytes 3145732
  180.1 4.3 %copy-start.42 = (f32[16,128,128]{1,2,0:T(8,128)S(1)}, f32[16,128,128]{1,2,0:T(8,128)}, u32[]{:S(2)}) copy-start(f32[16,128,128]{1,2,0:T(8,128)} %get-tuple-element.42) | copy-start | bytes 3145732
  190.7 6.3 %copy-start.10 = (f32[16,128,128]{1,2,0:T(8,128)S(1)}, f32[16,128,128]{1,2,0:T(8,128)}, u32[]{:S(2)}) copy-start(f32[16,128,128]{1,2,0:T(8,128)} %convolution_select_fusion.8) | copy-start | bytes 3145732
  192.7 11.8 %all-to-all-start.11 = ((bf16[16,2,4,16,128]{4,3,1,0,2:T(8,128)(2,1)}), bf16[16,2,4,16,128]{4,3,1,0,2:T(8,128)(2,1)}, u32[]{:S(2)}, u32[]{:S(2)}) async-start(bf16[16,2,4,16,128]{4,3,1,0,2:T(8,128)(2,1)} %copy.211), calls=%async_computation.11 | async-start | bytes 1048576 | tf_op jit(solution)/shard_map/all_to_all | solution.py:34
  197.0 9.1 %copy-start.3 = (bf16[1,1,2048,128]{3,2,1,0:T(8,128)(2,1)S(1)}, bf16[1,1,2048,128]{3,2,1,0:T(8,128)(2,1)}, u32[]{:S(2)}) copy-start(bf16[1,1,2048,128]{3,2,1,0:T(8,128)(2,1)} %copy-done.2) | copy-start | bytes 1572868
  (32 other events, 54.9 us)
where the time goes:
time: 214 us; the launch traced here: 212 us
  waiting for transfers between devices  53.1 us (25%)
  matrix products  48.6 us (23%)
  starting transfers between devices  48.2 us (23%)
  local copies, waits for them, and re-layouts  47.4 us (22%)
  blocking collectives  9.7 us (5%)
  other arithmetic  3.26 us (2%)
    all_to_all x5, waiting for transfers between devices, unpermute_blocks(): lax.all_to_all(shaped, 'tensor', split_axis=2, concat_axis=0, tiled=True)  28.8 us
    all_to_all x6, starting transfers between devices, permute_blocks(): lax.all_to_all(shaped, 'tensor', split_axis=2, concat_axis=1, tiled=True)  25.9 us
    all_to_all x6, waiting for transfers between devices, permute_blocks(): lax.all_to_all(shaped, 'tensor', split_axis=2, concat_axis=1, tiled=True)  24.3 us
    all_to_all x5, starting transfers between devices, unpermute_blocks(): lax.all_to_all(shaped, 'tensor', split_axis=2, concat_axis=0, tiled=True)  20.9 us
    dot_general x6, matrix products, shards(): jnp.einsum('kji,kjt->kit', first_local[layer_slot], returned, preferred_e...  12 us
    dot_general x6, matrix products, recompute(): jnp.einsum('kij,mkjt->mkit', factor_two[layer_slot], permuted, preferred_...  10.7 us
    unnamed x90, local copies, waits for them, and re-layouts  10.6 us
    dot_general x6, matrix products, shards(): jnp.einsum('kit,kjt->kij', returned, hidden, preferred_element_type=jnp.f...  10.1 us
  transfers between devices with their start and end apart: 12, of which 11 were waited for; matrix products, arithmetic and copies ran while one was open for 16% of the time, Pallas kernels for 0%

commit v1 on v0

--- a/solution.py
+++ b/solution.py
@@ -1,6 +1,10 @@
+import functools
+
 import jax
 import jax.numpy as jnp
 from jax import lax
+from jax.experimental import pallas as pl
+from jax.experimental.pallas import tpu as pltpu
 from jax.sharding import PartitionSpec as P
 
 
@@ -135,6 +139,384 @@
     return (last_emitted, first_out, second_out, gate_out)
 
 
+MESH = pl.DeviceIdType.MESH
+F32 = jnp.float32
+BF16 = jnp.bfloat16
+CHUNKS = 4
+
+
+def kernel(
+    inp, arr, loss, one, two, gate, count_ref,
+    emit_out, first_out, second_out, gate_out,
+    hid, perm, ret, send_f, send_b, work, slope, silu, gate_b, grad, gate_acc, scaled,
+    hop_in, hop_out,
+    recv_f, recv_b, sent_f, sent_b, hop_recv, hop_sent, loss_sem,
+):
+    slots, blocks, size, tokens = one.shape
+    rows = perm.shape[1]
+    repeat = rows // blocks
+    per = blocks // CHUNKS
+    span = rows // CHUNKS
+    me = lax.axis_index("tensor")
+    section = lax.axis_index("section")
+    last = lax.axis_size("section") - 1
+    me_low, me_high = me % 2, me // 2
+
+    def partner(d):
+        low = 1 - me_low if d % 2 else me_low
+        high = 1 - me_high if d // 2 else me_high
+        return high * 2 + low
+
+    barrier = pltpu.get_barrier_semaphore()
+    for d in (1, 2, 3):
+        pl.semaphore_signal(
+            barrier, inc=1, device_id={"tensor": partner(d)}, device_id_type=MESH
+        )
+
+    @pl.when(section > 0)
+    def _():
+        pl.semaphore_signal(barrier, inc=1, device_id={"section": section - 1}, device_id_type=MESH)
+
+    @pl.when(section < last)
+    def _():
+        pl.semaphore_signal(barrier, inc=1, device_id={"section": section + 1}, device_id_type=MESH)
+
+    @pl.when(section == last)
+    def _():
+        pltpu.make_async_copy(loss, hop_in, loss_sem).start()
+
+    count = count_ref[0]
+
+    def hidden(t, l):
+        return inp.at[t] if l == 0 else hid.at[t, l - 1]
+
+    def step(t, l):
+        return t * slots + l
+
+    def dot(a, b):
+        return jnp.dot(a, b, preferred_element_type=F32)
+
+    def dot_t(a, b):
+        return lax.dot_general(a, b, (((0,), (0,)), ((), ())), preferred_element_type=F32)
+
+    def work_rows(k):
+        return pl.ds(pl.multiple_of(k * size, size), size)
+
+    def each_chunk(body):
+        lax.fori_loop(0, CHUNKS, lambda c, _: (body(c), 0)[1], 0)
+
+    def each_block(body):
+        def chunk(c):
+            for b in range(per):
+                body(c * per + b)
+
+        each_chunk(chunk)
+
+    def copy_f(f, d, c, source):
+        part = pl.ds(c * span, span)
+        return pltpu.make_async_remote_copy(
+            src_ref=send_f.at[f, d - 1, part],
+            dst_ref=perm.at[f, part, source],
+            send_sem=sent_f.at[f, d - 1],
+            recv_sem=recv_f.at[f, c, d - 1],
+            device_id={"tensor": partner(d)},
+            device_id_type=MESH,
+        )
+
+    def copy_b(f, d, c, source):
+        part = pl.ds(c * per, per)
+        return pltpu.make_async_remote_copy(
+            src_ref=send_b.at[f, d - 1, part],
+            dst_ref=ret.at[f, part, source],
+            send_sem=sent_b.at[f, d - 1],
+            recv_sem=recv_b.at[f, c, d - 1],
+            device_id={"tensor": partner(d)},
+            device_id_type=MESH,
+        )
+
+    def scatter_f(f):
+        def chunk(c):
+            for d in (3, 1, 2, 0):
+                target = partner(d)
+                for j in range(span):
+                    row = c * span + j
+                    tile = work[pl.ds(target * rows + row, blocks, stride=size), :].astype(BF16)
+                    if d:
+                        send_f[f, d - 1, row] = tile
+                    else:
+                        perm[f, row, me] = tile
+                if d:
+                    copy_f(f, d, c, me).start()
+
+        each_chunk(chunk)
+
+    def scatter_b(f):
+        def chunk(c):
+            for d in (3, 1, 2, 0):
+                target = partner(d)
+                for j in range(per):
+                    block = c * per + j
+                    tile = work[
+                        pl.ds(target * blocks + block, rows, stride=size // repeat), :
+                    ].astype(BF16)
+                    if d:
+                        send_b[f, d - 1, block] = tile
+                    else:
+                        ret[f, block, me] = tile
+                if d:
+                    copy_b(f, d, c, me).start()
+
+        each_chunk(chunk)
+
+    def permuted(f, k):
+        return perm[f, pl.ds(k * repeat, repeat)].reshape(size, tokens)
+
+    def back(t, l, k, value):
+        f = step(t, l)
+        rounded = (value * slope[f, k]).astype(BF16)
+        scaled[f, k] = rounded
+        work[work_rows(k), :] = dot_t(two[l, k], rounded)
+        grad[k] = value
+        product = value * silu[f, k]
+        gate_acc[l, k] = product if t == 0 else gate_acc[l, k] + product
+
+    def forward(t, l, then):
+        f = step(t, l)
+
+        def chunk(c):
+            for d in (1, 2, 3):
+                copy_f(f, d, c, partner(d)).wait_recv()
+            for b in range(per):
+                k = c * per + b
+                mixed = dot(two[l, k], permuted(f, k))
+                logistic = 0.5 + 0.5 * jnp.tanh(0.5 * mixed)
+                branch = mixed * logistic
+                scale = gate_b[l, k]
+                if l + 1 < slots:
+                    old = hidden(t, l)[k].astype(F32)
+                    new = jnp.where(l < count, old + scale * branch, old).astype(BF16)
+                    hid[t, l, k] = new
+                    work[work_rows(k), :] = dot(one[l + 1, k], new)
+                silu[f, k] = branch
+                slope[f, k] = scale * (logistic * (1.0 + mixed * (1.0 - logistic)))
+                if then is not None:
+                    then(k)
+
+        each_chunk(chunk)
+
+    def backward(t, l, then):
+        f = step(t, l)
+
+        def chunk(c):
+            for d in (1, 2, 3):
+                copy_b(f, d, c, partner(d)).wait_recv()
+            for b in range(per):
+                k = c * per + b
+                term = dot_t(one[l, k], ret[f, k].reshape(size, tokens))
+                value = jnp.where(l < count, grad[k] + term, grad[k])
+                then(k, value)
+            if t == 0 and l == 0:
+                hop_send(c)
+
+        each_chunk(chunk)
+
+    def hop_copy(c):
+        part = pl.ds(c * per, per)
+        return pltpu.make_async_remote_copy(
+            src_ref=hop_out.at[part],
+            dst_ref=hop_in.at[part],
+            send_sem=hop_sent.at[c],
+            recv_sem=hop_recv.at[c],
+            device_id={"section": section - 1},
+            device_id_type=MESH,
+        )
+
+    def hop_send(c):
+        @pl.when(section > 0)
+        def _():
+            hop_copy(c).start()
+
+    def second_grads(l):
+        f, g = step(0, l), step(1, l)
+
+        def block(k):
+            left = jnp.concatenate([scaled[f, k], scaled[g, k]], axis=1)
+            right = jnp.concatenate([permuted(f, k), permuted(g, k)], axis=1)
+            total = lax.dot_general(left, right, (((1,), (1,)), ((), ())), preferred_element_type=F32)
+            second_out[l, k] = jnp.where(l < count, total, 0.0).astype(BF16)
+            gates = jnp.sum(gate_acc[l, k].T, axis=0, keepdims=True)
+            gate_out[l, pl.ds(k, 1), :] = jnp.where(l < count, gates, 0.0)
+
+        each_block(block)
+
+    def first_grads(l):
+        f, g = step(0, l), step(1, l)
+
+        def block(k):
+            left = jnp.concatenate(
+                [ret[f, k].reshape(size, tokens), ret[g, k].reshape(size, tokens)], axis=1
+            )
+            right = jnp.concatenate([hidden(0, l)[k], hidden(1, l)[k]], axis=1)
+            total = lax.dot_general(left, right, (((1,), (1,)), ((), ())), preferred_element_type=F32)
+            first_out[l, k] = jnp.where(l < count, total, 0.0).astype(BF16)
+
+        each_block(block)
+
+    def start(t):
+        def block(k):
+            work[work_rows(k), :] = dot(one[0, k], inp[t, k])
+
+        each_block(block)
+
+    def widen(l):
+        def block(k):
+            gate_b[l, k] = jnp.broadcast_to(gate[l, pl.ds(k, 1), :], (size, size)).T
+
+        each_block(block)
+
+    start(0)
+    pl.semaphore_wait(
+        barrier, 3 + jnp.where(section > 0, 1, 0) + jnp.where(section < last, 1, 0)
+    )
+    scatter_f(step(0, 0))
+    start(1)
+    scatter_f(step(1, 0))
+    for l in range(slots):
+        widen(l)
+    top = slots - 1
+    for l in range(top):
+        for t in (0, 1):
+            forward(t, l, None)
+            scatter_f(step(t, l + 1))
+    forward(0, top, lambda k: back(0, top, k, arr[k].astype(F32)))
+    scatter_b(step(0, top))
+    forward(1, top, None)
+    for l in range(top, 0, -1):
+        backward(0, l, functools.partial(back, 0, l - 1))
+        scatter_b(step(0, l - 1))
+
+    def leave(k, value):
+        hop_out[k] = value.astype(BF16)
+
+    backward(0, 0, leave)
+
+    @pl.when(section == last)
+    def _():
+        pltpu.make_async_copy(loss, hop_in, loss_sem).wait()
+
+    def arrive(c):
+        @pl.when(section < last)
+        def _():
+            hop_copy(c).wait_recv()
+
+        for b in range(per):
+            k = c * per + b
+            back(1, top, k, hop_in[k].astype(F32))
+
+    each_chunk(arrive)
+    scatter_b(step(1, top))
+    for l in range(top, 0, -1):
+        second_grads(l)
+        if l < top:
+            first_grads(l + 1)
+        backward(1, l, functools.partial(back, 1, l - 1))
+        scatter_b(step(1, l - 1))
+    second_grads(0)
+    if top > 0:
+        first_grads(1)
+
+    def emit(k, value):
+        emit_out[k] = value.astype(BF16)
+
+    backward(1, 0, emit)
+    first_grads(0)
+
+    for t in (0, 1):
+        for l in range(slots):
+            f = step(t, l)
+            for d in (1, 2, 3):
+                pltpu.make_async_remote_copy(
+                    src_ref=send_f.at[f, d - 1], dst_ref=perm.at[f, :, me],
+                    send_sem=sent_f.at[f, d - 1], recv_sem=recv_f.at[f, 0, d - 1],
+                    device_id={"tensor": partner(d)}, device_id_type=MESH,
+                ).wait_send()
+                pltpu.make_async_remote_copy(
+                    src_ref=send_b.at[f, d - 1], dst_ref=ret.at[f, :, me],
+                    send_sem=sent_b.at[f, d - 1], recv_sem=recv_b.at[f, 0, d - 1],
+                    device_id={"tensor": partner(d)}, device_id_type=MESH,
+                ).wait_send()
+
+    @pl.when(section > 0)
+    def _():
+        each_chunk(lambda c: hop_copy(c).wait_send())
+
+
+def fused_shards(
+    section_inputs, arriving_grad, loss_grad, factor_first, factor_second, gate_scales, layer_count
+):
+    moments = section_inputs.shape[1]
+    _, slots, blocks, size, _ = factor_first.shape
+    tokens = section_inputs.shape[3]
+    tensor = lax.axis_size("tensor")
+    rows = size // tensor
+    steps = moments * slots
+    vmem = pl.BlockSpec(memory_space=pltpu.VMEM)
+    block = (blocks, size, tokens)
+    factor = (slots, blocks, size, size)
+    outs = pl.pallas_call(
+        kernel,
+        out_shape=[
+            jax.ShapeDtypeStruct(block, BF16),
+            jax.ShapeDtypeStruct(factor, BF16),
+            jax.ShapeDtypeStruct(factor, BF16),
+            jax.ShapeDtypeStruct((slots, blocks, size), F32),
+        ],
+        in_specs=[vmem] * 6 + [pl.BlockSpec(memory_space=pltpu.SMEM)],
+        out_specs=[vmem] * 4,
+        scratch_shapes=[
+            pltpu.VMEM((moments, max(slots - 1, 1)) + block, BF16),
+            pltpu.VMEM((steps, rows, tensor, blocks, tokens), BF16),
+            pltpu.VMEM((steps, blocks, tensor, rows, tokens), BF16),
+            pltpu.VMEM((steps, 3, rows, blocks, tokens), BF16),
+            pltpu.VMEM((steps, 3, blocks, rows, tokens), BF16),
+            pltpu.VMEM((blocks * size, tokens), F32),
+            pltpu.VMEM((steps,) + block, F32),
+            pltpu.VMEM((steps,) + block, F32),
+            pltpu.VMEM((slots,) + block, F32),
+            pltpu.VMEM(block, F32),
+            pltpu.VMEM((slots,) + block, F32),
+            pltpu.VMEM((steps,) + block, BF16),
+            pltpu.VMEM(block, BF16),
+            pltpu.VMEM(block, BF16),
+            pltpu.SemaphoreType.DMA((steps, CHUNKS, 3)),
+            pltpu.SemaphoreType.DMA((steps, CHUNKS, 3)),
+            pltpu.SemaphoreType.DMA((steps, 3)),
+            pltpu.SemaphoreType.DMA((steps, 3)),
+            pltpu.SemaphoreType.DMA((CHUNKS,)),
+            pltpu.SemaphoreType.DMA((CHUNKS,)),
+            pltpu.SemaphoreType.DMA(()),
+        ],
+        compiler_params=pltpu.CompilerParams(
+            collective_id=0, has_side_effects=True, vmem_limit_bytes=56 * 1024 * 1024
+        ),
+    )(
+        section_inputs[0].reshape((moments,) + block),
+        arriving_grad[0].reshape(block),
+        loss_grad[0].reshape(block),
+        factor_first[0],
+        factor_second[0],
+        gate_scales[0].reshape(slots, blocks, size),
+        layer_count,
+    )
+    emitted, first_grad, second_grad, gate_grad = outs
+    return (
+        emitted.reshape(1, blocks * size, tokens),
+        first_grad[None],
+        second_grad[None],
+        gate_grad.reshape(1, slots, blocks * size),
+    )
+
+
 def solution(mesh):
     in_specs = (
         P("section", None, "tensor", None),
@@ -151,4 +533,5 @@
         P("section", None, "tensor", None, None),
         P("section", None, "tensor"),
     )
-    return jax.shard_map(shards, mesh=mesh, in_specs=in_specs, out_specs=out_specs, check_vma=False)
+    fused = mesh.shape["tensor"] == 4
+    return jax.shard_map(fused_shards if fused else shards, mesh=mesh, in_specs=in_specs, out_specs=out_specs, check_vma=False)

time: 214 us -> 101 us (0.47)
  the two profiles are of different devices: /device:TPU:0 before, /device:TPU:1 now
where the time goes in v1:
time: 101 us; the launch traced here: 100 us
  Pallas kernels  92.6 us (92%)
  local copies, waits for them, and re-layouts  6.47 us (6%)
  between operations  1.29 us (1%)
    pallas_call x1, Pallas kernels, fused_shards(): pl.pallas_call(kernel, out_shape=[jax.ShapeDtypeStruct(block, BF16), jax....  92.6 us
    unnamed x8, local copies, waits for them, and re-layouts  6.47 us

profile of v1, /device:TPU:1, one launch (start us, length us, event | category | flops | bytes accessed | tf_op | source)
XLA Modules:
  0.0 100.4 jit_solution(17599749962530013848)
XLA Ops:
  1.3 92.6 %shard_map.102 = (bf16[16,128,128]{2,1,0:T(8,128)(2,1)}, bf16[3,16,128,128]{3,2,1,0:T(8,128)(2,1)}, bf16[3,16,128,128]{3,2,1,0:T(8,128)(2,1)}, f32[3,16,128]{2,1,0:T(8,128)}) custom-call(bf16[2,16,128,128]{3,2,1,0:T(8,128)(2,1)} %bitcast.14, bf16[16,128,128]{2,1,0:T(8,128)(2,1)} %bitcast.16, bf16[16,128,128]{2,1,0:T(8,128)(2,1)} %bitcast.17, ...), custom_call_target="tpu_custom_call" | custom-call | tf_op jit(solution)/shard_map/pallas_call | solution.py:466
  93.9 1.9 %copy.18 = bf16[1,2048,128]{2,1,0:T(8,128)(2,1)} copy(bf16[1,2048,128]{2,1,0:T(8,128)(2,1)} %bitcast.15) | data formatting | bytes 1048576
  95.8 0.0 copy-start
  95.8 2.8 %copy.19 = bf16[1,3,16,128,128]{4,3,2,1,0:T(8,128)(2,1)} copy(bf16[1,3,16,128,128]{4,3,2,1,0:T(8,128)(2,1)} %bitcast.11) | data formatting | bytes 3145728
  98.6 0.0 copy-done
  98.6 0.0 copy-start.1
  98.6 1.1 %copy.20 = bf16[1,3,16,128,128]{4,3,2,1,0:T(8,128)(2,1)} copy(bf16[1,3,16,128,128]{4,3,2,1,0:T(8,128)(2,1)S(1)} %bitcast.10) | data formatting | bytes 3145728
  99.8 0.0 copy-done.1
  99.8 0.6 copy.21
Async XLA Ops:
  95.8 2.9 %copy-start = (bf16[3,16,128,128]{3,2,1,0:T(8,128)(2,1)S(1)}, bf16[3,16,128,128]{3,2,1,0:T(8,128)(2,1)}, u32[]{:S(2)}) copy-start(bf16[3,16,128,128]{3,2,1,0:T(8,128)(2,1)} %get-tuple-element.10) | copy-start | bytes 4718596
  98.6 1.1 %copy-start.1 = (f32[3,16,128]{2,1,0:T(8,128)S(1)}, f32[3,16,128]{2,1,0:T(8,128)}, u32[]{:S(2)}) copy-start(f32[3,16,128]{2,1,0:T(8,128)} %get-tuple-element.11) | copy-start | bytes 73732

commit v2 on v1

--- a/solution.py
+++ b/solution.py
@@ -146,11 +146,12 @@
 
 
 def kernel(
-    inp, arr, loss, one, two, gate, count_ref,
+    inp_far, arr_far, loss, one_far, two_far, gate_far, count_ref,
     emit_out, first_out, second_out, gate_out,
-    hid, perm, ret, send_f, send_b, work, slope, silu, gate_b, grad, gate_acc, scaled,
+    inp, arr, one, two, gate, hid, perm, ret, send_f, send_b, work, slope, silu, gate_b, grad, gate_acc, scaled,
     hop_in, hop_out,
     recv_f, recv_b, sent_f, sent_b, hop_recv, hop_sent, loss_sem,
+    inp_sem, one_sem, two_sem, far_sem,
 ):
     slots, blocks, size, tokens = one.shape
     rows = perm.shape[1]
@@ -166,6 +167,27 @@
         low = 1 - me_low if d % 2 else me_low
         high = 1 - me_high if d // 2 else me_high
         return high * 2 + low
+
+    def load_inp(t):
+        return pltpu.make_async_copy(inp_far.at[t], inp.at[t], inp_sem.at[t])
+
+    def load_one(l):
+        return pltpu.make_async_copy(one_far.at[l], one.at[l], one_sem.at[l])
+
+    def load_two(l):
+        return pltpu.make_async_copy(two_far.at[l], two.at[l], two_sem.at[l])
+
+    load_gate = pltpu.make_async_copy(gate_far, gate, far_sem.at[0])
+    load_arr = pltpu.make_async_copy(arr_far, arr, far_sem.at[1])
+    load_inp(0).start()
+    load_one(0).start()
+    load_inp(1).start()
+    load_gate.start()
+    for l in range(slots):
+        load_two(l).start()
+        if l:
+            load_one(l).start()
+    load_arr.start()
 
     barrier = pltpu.get_barrier_semaphore()
     for d in (1, 2, 3):
@@ -315,6 +337,8 @@
                 term = dot_t(one[l, k], ret[f, k].reshape(size, tokens))
                 value = jnp.where(l < count, grad[k] + term, grad[k])
                 then(k, value)
+                if t == 1 and l == 0:
+                    first_grad(0, k)
             if t == 0 and l == 0:
                 hop_send(c)
 
@@ -349,10 +373,8 @@
 
         each_block(block)
 
-    def first_grads(l):
-        f, g = step(0, l), step(1, l)
-
-        def block(k):
+    def first_grad(l, k):
+            f, g = step(0, l), step(1, l)
             left = jnp.concatenate(
                 [ret[f, k].reshape(size, tokens), ret[g, k].reshape(size, tokens)], axis=1
             )
@@ -360,7 +382,8 @@
             total = lax.dot_general(left, right, (((1,), (1,)), ((), ())), preferred_element_type=F32)
             first_out[l, k] = jnp.where(l < count, total, 0.0).astype(BF16)
 
-        each_block(block)
+    def first_grads(l):
+        each_block(functools.partial(first_grad, l))
 
     def start(t):
         def block(k):
@@ -374,15 +397,23 @@
 
         each_block(block)
 
+    load_inp(0).wait()
+    load_one(0).wait()
     start(0)
     pl.semaphore_wait(
         barrier, 3 + jnp.where(section > 0, 1, 0) + jnp.where(section < last, 1, 0)
     )
     scatter_f(step(0, 0))
+    load_inp(1).wait()
     start(1)
     scatter_f(step(1, 0))
+    load_gate.wait()
     for l in range(slots):
         widen(l)
+        load_two(l).wait()
+        if l:
+            load_one(l).wait()
+    load_arr.wait()
     top = slots - 1
     for l in range(top):
         for t in (0, 1):
@@ -429,7 +460,6 @@
         emit_out[k] = value.astype(BF16)
 
     backward(1, 0, emit)
-    first_grads(0)
 
     for t in (0, 1):
         for l in range(slots):
@@ -449,6 +479,29 @@
     @pl.when(section > 0)
     def _():
         each_chunk(lambda c: hop_copy(c).wait_send())
+
+
+def store_kernel(*refs):
+    count = len(refs) // 2
+    sems = refs[-1]
+    copies = [
+        pltpu.make_async_copy(refs[i], refs[count + i], sems.at[i]) for i in range(count)
+    ]
+    for copy in copies:
+        copy.start()
+    for copy in copies:
+        copy.wait()
+
+
+def store(values):
+    return pl.pallas_call(
+        store_kernel,
+        out_shape=[jax.ShapeDtypeStruct(v.shape, v.dtype) for v in values],
+        in_specs=[pl.BlockSpec(memory_space=pltpu.VMEM)] * len(values),
+        out_specs=[pl.BlockSpec(memory_space=pl.ANY)] * len(values),
+        scratch_shapes=[pltpu.SemaphoreType.DMA((len(values),))],
+        compiler_params=pltpu.CompilerParams(vmem_limit_bytes=8 * 1024 * 1024),
+    )(*values)
 
 
 def fused_shards(
@@ -466,14 +519,19 @@
     outs = pl.pallas_call(
         kernel,
         out_shape=[
-            jax.ShapeDtypeStruct(block, BF16),
-            jax.ShapeDtypeStruct(factor, BF16),
-            jax.ShapeDtypeStruct(factor, BF16),
-            jax.ShapeDtypeStruct((slots, blocks, size), F32),
+            pltpu.VMEM(block, BF16),
+            pltpu.VMEM(factor, BF16),
+            pltpu.VMEM(factor, BF16),
+            pltpu.VMEM((slots, blocks, size), F32),
         ],
-        in_specs=[vmem] * 6 + [pl.BlockSpec(memory_space=pltpu.SMEM)],
+        in_specs=[pl.BlockSpec(memory_space=pl.ANY)] * 6 + [pl.BlockSpec(memory_space=pltpu.SMEM)],
         out_specs=[vmem] * 4,
         scratch_shapes=[
+            pltpu.VMEM((moments,) + block, BF16),
+            pltpu.VMEM(block, BF16),
+            pltpu.VMEM(factor, BF16),
+            pltpu.VMEM(factor, BF16),
+            pltpu.VMEM((slots, blocks, size), F32),
             pltpu.VMEM((moments, max(slots - 1, 1)) + block, BF16),
             pltpu.VMEM((steps, rows, tensor, blocks, tokens), BF16),
             pltpu.VMEM((steps, blocks, tensor, rows, tokens), BF16),
@@ -495,6 +553,10 @@
             pltpu.SemaphoreType.DMA((CHUNKS,)),
             pltpu.SemaphoreType.DMA((CHUNKS,)),
             pltpu.SemaphoreType.DMA(()),
+            pltpu.SemaphoreType.DMA((moments,)),
+            pltpu.SemaphoreType.DMA((slots,)),
+            pltpu.SemaphoreType.DMA((slots,)),
+            pltpu.SemaphoreType.DMA((2,)),
         ],
         compiler_params=pltpu.CompilerParams(
             collective_id=0, has_side_effects=True, vmem_limit_bytes=56 * 1024 * 1024
@@ -508,7 +570,7 @@
         gate_scales[0].reshape(slots, blocks, size),
         layer_count,
     )
-    emitted, first_grad, second_grad, gate_grad = outs
+    emitted, first_grad, second_grad, gate_grad = store(outs)
     return (
         emitted.reshape(1, blocks * size, tokens),
         first_grad[None],

time: 101 us -> 90.4 us (0.90)
  local copies, waits for them, and re-layouts: 6.47 us -> 0 us
  Pallas kernels: 92.6 us -> 88.9 us
    unnamed x8 -> x0, local copies, waits for them, and re-layouts: 6.47 us -> none
    pallas_call x1 -> x2, Pallas kernels: 92.6 us -> 88.9 us  [the longest x1 87 us: fused_shards(): pl.pallas_call(kernel, out_shape=[pltpu.VMEM(block, BF16), pltpu.VMEM(fac...]
where the time goes in v2:
time: 90.4 us; the launch traced here: 90.2 us
  Pallas kernels  88.9 us (98%)
  between operations  1.29 us (1%)
    pallas_call x1, Pallas kernels, fused_shards(): pl.pallas_call(kernel, out_shape=[pltpu.VMEM(block, BF16), pltpu.VMEM(fac...  87 us
    pallas_call x1, Pallas kernels, store(): pl.pallas_call(store_kernel, out_shape=[jax.ShapeDtypeStruct(v.shape, v.d...  1.87 us

profile of v2, /device:TPU:1, one launch (start us, length us, event | category | flops | bytes accessed | tf_op | source)
XLA Modules:
  0.0 90.2 jit_solution(16900352864808361852)
XLA Ops:
  1.3 87.0 %shard_map.102 = (bf16[16,128,128]{2,1,0:T(8,128)(2,1)S(1)}, bf16[3,16,128,128]{3,2,1,0:T(8,128)(2,1)S(1)}, bf16[3,16,128,128]{3,2,1,0:T(8,128)(2,1)S(1)}, f32[3,16,128]{2,1,0:T(8,128)S(1)}) custom-call(bf16[2,16,128,128]{3,2,1,0:T(8,128)(2,1)} %bitcast.12, bf16[16,128,128]{2,1,0:T(8,128)(2,1)} %bitcast.13, bf16[16,128,128]{2,1,0:T(8,128)(2,1)} %bitcast.14, ...), custom_call_target="tpu_custom_call" | custom-call | tf_op jit(solution)/shard_map/pallas_call | solution.py:519
  88.3 1.9 %shard_map.103 = (bf16[16,128,128]{2,1,0:T(8,128)(2,1)}, bf16[3,16,128,128]{3,2,1,0:T(8,128)(2,1)}, bf16[3,16,128,128]{3,2,1,0:T(8,128)(2,1)}, f32[3,16,128]{2,1,0:T(8,128)}) custom-call(bf16[16,128,128]{2,1,0:T(8,128)(2,1)S(1)} %get-tuple-element.12.refs_0_, bf16[3,16,128,128]{3,2,1,0:T(8,128)(2,1)S(1)} %get-tuple-element.13.refs_1_, ...), custom_call_target="tpu_custom_call" | custom-call | tf_op jit(solution)/shard_map/pallas_call | solution.py:497

commit v3 on v2

--- a/solution.py
+++ b/solution.py
@@ -224,8 +224,21 @@
     def work_rows(k):
         return pl.ds(pl.multiple_of(k * size, size), size)
 
-    def each_chunk(body):
-        lax.fori_loop(0, CHUNKS, lambda c, _: (body(c), 0)[1], 0)
+    def each_chunk(body, low=0, high=CHUNKS):
+        lax.fori_loop(low, high, lambda c, _: (body(c), 0)[1], 0)
+
+    def room(t, l):
+        return 0 if t == 0 else 1 + l % 2
+
+    def beside(chunk, early, late):
+        def body(c):
+            if early is not None:
+                pl.when(c == CHUNKS // 2)(early)
+            if late is not None:
+                pl.when(c == CHUNKS - 1)(late)
+            chunk(c)
+
+        each_chunk(body)
 
     def each_block(body):
         def chunk(c):
@@ -256,13 +269,17 @@
             device_id_type=MESH,
         )
 
-    def scatter_f(f):
+    def scatter_f(t, l, low=0, high=CHUNKS):
+        f = step(t, l)
+
         def chunk(c):
             for d in (3, 1, 2, 0):
                 target = partner(d)
                 for j in range(span):
                     row = c * span + j
-                    tile = work[pl.ds(target * rows + row, blocks, stride=size), :].astype(BF16)
+                    tile = work[
+                        room(t, l), pl.ds(target * rows + row, blocks, stride=size), :
+                    ].astype(BF16)
                     if d:
                         send_f[f, d - 1, row] = tile
                     else:
@@ -270,7 +287,7 @@
                 if d:
                     copy_f(f, d, c, me).start()
 
-        each_chunk(chunk)
+        each_chunk(chunk, low, high)
 
     def scatter_b(f):
         def chunk(c):
@@ -279,7 +296,7 @@
                 for j in range(per):
                     block = c * per + j
                     tile = work[
-                        pl.ds(target * blocks + block, rows, stride=size // repeat), :
+                        0, pl.ds(target * blocks + block, rows, stride=size // repeat), :
                     ].astype(BF16)
                     if d:
                         send_b[f, d - 1, block] = tile
@@ -297,12 +314,12 @@
         f = step(t, l)
         rounded = (value * slope[f, k]).astype(BF16)
         scaled[f, k] = rounded
-        work[work_rows(k), :] = dot_t(two[l, k], rounded)
+        work[0, work_rows(k), :] = dot_t(two[l, k], rounded)
         grad[k] = value
         product = value * silu[f, k]
         gate_acc[l, k] = product if t == 0 else gate_acc[l, k] + product
 
-    def forward(t, l, then):
+    def forward(t, l, then, early=None, late=None, low=0, high=CHUNKS):
         f = step(t, l)
 
         def chunk(c):
@@ -318,15 +335,18 @@
                     old = hidden(t, l)[k].astype(F32)
                     new = jnp.where(l < count, old + scale * branch, old).astype(BF16)
                     hid[t, l, k] = new
-                    work[work_rows(k), :] = dot(one[l + 1, k], new)
+                    work[room(t, l + 1), work_rows(k), :] = dot(one[l + 1, k], new)
                 silu[f, k] = branch
                 slope[f, k] = scale * (logistic * (1.0 + mixed * (1.0 - logistic)))
                 if then is not None:
                     then(k)
 
-        each_chunk(chunk)
-
-    def backward(t, l, then):
+        if low or high < CHUNKS:
+            each_chunk(chunk, low, high)
+        else:
+            beside(chunk, early, late)
+
+    def backward(t, l, then, early=None, late=None):
         f = step(t, l)
 
         def chunk(c):
@@ -342,7 +362,7 @@
             if t == 0 and l == 0:
                 hop_send(c)
 
-        each_chunk(chunk)
+        beside(chunk, early, late)
 
     def hop_copy(c):
         part = pl.ds(c * per, per)
@@ -387,7 +407,7 @@
 
     def start(t):
         def block(k):
-            work[work_rows(k), :] = dot(one[0, k], inp[t, k])
+            work[room(t, 0), work_rows(k), :] = dot(one[0, k], inp[t, k])
 
         each_block(block)
 
@@ -403,33 +423,54 @@
     pl.semaphore_wait(
         barrier, 3 + jnp.where(section > 0, 1, 0) + jnp.where(section < last, 1, 0)
     )
-    scatter_f(step(0, 0))
+    scatter_f(0, 0)
     load_inp(1).wait()
     start(1)
-    scatter_f(step(1, 0))
     load_gate.wait()
-    for l in range(slots):
-        widen(l)
-        load_two(l).wait()
-        if l:
-            load_one(l).wait()
+    widen(0)
+    load_two(0).wait()
+
+    half = CHUNKS // 2
+    halves = [(0, half), (half, CHUNKS)]
+    turns = [(l, h) for l in range(slots) for h in halves]
+
+    def receive(n):
+        if n <= 0 or n > len(turns):
+            return None
+        l, (low, high) = turns[n - 1]
+        return lambda: forward(1, l, None, low=low, high=high)
+
+    def send(n):
+        if n >= len(turns):
+            return None
+        l, (low, high) = turns[n]
+        return lambda: scatter_f(1, l, low, high)
+
+    top = slots - 1
+    turn = 0
+    for l in range(top):
+        load_one(l + 1).wait()
+        forward(0, l, None, receive(turn), send(turn))
+        turn += 1
+        scatter_f(0, l + 1)
+        widen(l + 1)
+        load_two(l + 1).wait()
     load_arr.wait()
-    top = slots - 1
-    for l in range(top):
-        for t in (0, 1):
-            forward(t, l, None)
-            scatter_f(step(t, l + 1))
-    forward(0, top, lambda k: back(0, top, k, arr[k].astype(F32)))
+    forward(
+        0, top, lambda k: back(0, top, k, arr[k].astype(F32)), receive(turn), send(turn)
+    )
+    turn += 1
     scatter_b(step(0, top))
-    forward(1, top, None)
     for l in range(top, 0, -1):
-        backward(0, l, functools.partial(back, 0, l - 1))
+        backward(0, l, functools.partial(back, 0, l - 1), receive(turn), send(turn))
+        turn += 1
         scatter_b(step(0, l - 1))
 
     def leave(k, value):
         hop_out[k] = value.astype(BF16)
 
-    backward(0, 0, leave)
+    backward(0, 0, leave, receive(turn), send(turn))
+    turn += 1
 
     @pl.when(section == last)
     def _():
@@ -444,7 +485,7 @@
             k = c * per + b
             back(1, top, k, hop_in[k].astype(F32))
 
-    each_chunk(arrive)
+    beside(arrive, receive(turn), None)
     scatter_b(step(1, top))
     for l in range(top, 0, -1):
         second_grads(l)
@@ -537,7 +578,7 @@
             pltpu.VMEM((steps, blocks, tensor, rows, tokens), BF16),
             pltpu.VMEM((steps, 3, rows, blocks, tokens), BF16),
             pltpu.VMEM((steps, 3, blocks, rows, tokens), BF16),
-            pltpu.VMEM((blocks * size, tokens), F32),
+            pltpu.VMEM((3, blocks * size, tokens), F32),
             pltpu.VMEM((steps,) + block, F32),
             pltpu.VMEM((steps,) + block, F32),
             pltpu.VMEM((slots,) + block, F32),

time: 90.4 us -> 89.9 us (level)
  the two profiles are of different devices: /device:TPU:1 before, /device:TPU:0 now
where the time goes in v3:
time: 89.9 us; the launch traced here: 89.7 us
  Pallas kernels  88.5 us (98%)
  between operations  1.29 us (1%)
    pallas_call x1, Pallas kernels, fused_shards(): pl.pallas_call(kernel, out_shape=[pltpu.VMEM(block, BF16), pltpu.VMEM(fac...  86.6 us
    pallas_call x1, Pallas kernels, store(): pl.pallas_call(store_kernel, out_shape=[jax.ShapeDtypeStruct(v.shape, v.d...  1.87 us

profile of v3, /device:TPU:0, one launch (start us, length us, event | category | flops | bytes accessed | tf_op | source)
XLA Modules:
  0.0 89.7 jit_solution(16722818855066891716)
XLA Ops:
  1.3 86.6 %shard_map.102 = (bf16[16,128,128]{2,1,0:T(8,128)(2,1)S(1)}, bf16[3,16,128,128]{3,2,1,0:T(8,128)(2,1)S(1)}, bf16[3,16,128,128]{3,2,1,0:T(8,128)(2,1)S(1)}, f32[3,16,128]{2,1,0:T(8,128)S(1)}) custom-call(bf16[2,16,128,128]{3,2,1,0:T(8,128)(2,1)} %bitcast.12, bf16[16,128,128]{2,1,0:T(8,128)(2,1)} %bitcast.13, bf16[16,128,128]{2,1,0:T(8,128)(2,1)} %bitcast.14, ...), custom_call_target="tpu_custom_call" | custom-call | tf_op jit(solution)/shard_map/pallas_call | solution.py:560
  87.9 1.9 %shard_map.103 = (bf16[16,128,128]{2,1,0:T(8,128)(2,1)}, bf16[3,16,128,128]{3,2,1,0:T(8,128)(2,1)}, bf16[3,16,128,128]{3,2,1,0:T(8,128)(2,1)}, f32[3,16,128]{2,1,0:T(8,128)}) custom-call(bf16[16,128,128]{2,1,0:T(8,128)(2,1)S(1)} %get-tuple-element.12.refs_0_, bf16[3,16,128,128]{3,2,1,0:T(8,128)(2,1)S(1)} %get-tuple-element.13.refs_1_, ...), custom_call_target="tpu_custom_call" | custom-call | tf_op jit(solution)/shard_map/pallas_call | solution.py:538

commit v4 on v3

--- a/solution.py
+++ b/solution.py
@@ -143,6 +143,7 @@
 F32 = jnp.float32
 BF16 = jnp.bfloat16
 CHUNKS = 4
+AHEAD = 2
 
 
 def kernel(
@@ -284,8 +285,10 @@
                         send_f[f, d - 1, row] = tile
                     else:
                         perm[f, row, me] = tile
-                if d:
+                if d and t:
                     copy_f(f, d, c, me).start()
+                elif d:
+                    pl.when(c < AHEAD)(copy_f(f, d, c, me).start)
 
         each_chunk(chunk, low, high)
 
@@ -303,7 +306,7 @@
                     else:
                         ret[f, block, me] = tile
                 if d:
-                    copy_b(f, d, c, me).start()
+                    pl.when(c < AHEAD)(copy_b(f, d, c, me).start)
 
         each_chunk(chunk)
 
@@ -325,6 +328,9 @@
         def chunk(c):
             for d in (1, 2, 3):
                 copy_f(f, d, c, partner(d)).wait_recv()
+            if t == 0:
+                for d in (3, 1, 2):
+                    pl.when(c + AHEAD < CHUNKS)(copy_f(f, d, c + AHEAD, me).start)
             for b in range(per):
                 k = c * per + b
                 mixed = dot(two[l, k], permuted(f, k))
@@ -352,6 +358,8 @@
         def chunk(c):
             for d in (1, 2, 3):
                 copy_b(f, d, c, partner(d)).wait_recv()
+            for d in (3, 1, 2):
+                pl.when(c + AHEAD < CHUNKS)(copy_b(f, d, c + AHEAD, me).start)
             for b in range(per):
                 k = c * per + b
                 term = dot_t(one[l, k], ret[f, k].reshape(size, tokens))

time: 89.9 us -> 101 us (1.12)
  Pallas kernels: 88.5 us -> 99.3 us
    pallas_call x1, Pallas kernels: 86.6 us -> 97.4 us  [fused_shards(): pl.pallas_call(kernel, out_shape=[pltpu.VMEM(block, BF16), pltpu.VMEM(fac...]
where the time goes in v4:
time: 101 us
  Pallas kernels  99.3 us (98%)
  between operations  1.29 us (1%)
    pallas_call x1, Pallas kernels, fused_shards(): pl.pallas_call(kernel, out_shape=[pltpu.VMEM(block, BF16), pltpu.VMEM(fac...  97.4 us

profile of v4, /device:TPU:0, one launch (start us, length us, event | category | flops | bytes accessed | tf_op | source)
XLA Modules:
  0.0 100.6 jit_solution(7671992702258696552)
XLA Ops:
  1.3 97.4 %shard_map.102 = (bf16[16,128,128]{2,1,0:T(8,128)(2,1)S(1)}, bf16[3,16,128,128]{3,2,1,0:T(8,128)(2,1)S(1)}, bf16[3,16,128,128]{3,2,1,0:T(8,128)(2,1)S(1)}, f32[3,16,128]{2,1,0:T(8,128)S(1)}) custom-call(bf16[2,16,128,128]{3,2,1,0:T(8,128)(2,1)} %bitcast.12, bf16[16,128,128]{2,1,0:T(8,128)(2,1)} %bitcast.13, bf16[16,128,128]{2,1,0:T(8,128)(2,1)} %bitcast.14, ...), custom_call_target="tpu_custom_call" | custom-call | tf_op jit(solution)/shard_map/pallas_call | solution.py:568
  98.7 1.9 %shard_map.103 = (bf16[16,128,128]{2,1,0:T(8,128)(2,1)}, bf16[3,16,128,128]{3,2,1,0:T(8,128)(2,1)}, bf16[3,16,128,128]{3,2,1,0:T(8,128)(2,1)}, f32[3,16,128]{2,1,0:T(8,128)}) custom-call(bf16[16,128,128]{2,1,0:T(8,128)(2,1)S(1)} %get-tuple-element.12.refs_0_, bf16[3,16,128,128]{3,2,1,0:T(8,128)(2,1)S(1)} %get-tuple-element.13.refs_1_, ...), custom_call_target="tpu_custom_call" | custom-call | tf_op jit(solution)/shard_map/pallas_call | solution.py:546

commit v5 on v3

--- a/solution.py
+++ b/solution.py
@@ -148,7 +148,7 @@
 def kernel(
     inp_far, arr_far, loss, one_far, two_far, gate_far, count_ref,
     emit_out, first_out, second_out, gate_out,
-    inp, arr, one, two, gate, hid, perm, ret, send_f, send_b, work, slope, silu, gate_b, grad, gate_acc, scaled,
+    inp, arr, one, two, one_t, two_t, gate, hid, perm, ret, send_f, send_b, work, slope, silu, gate_b, grad, gate_acc, scaled,
     hop_in, hop_out,
     recv_f, recv_b, sent_f, sent_b, hop_recv, hop_sent, loss_sem,
     inp_sem, one_sem, two_sem, far_sem,
@@ -218,8 +218,6 @@
     def dot(a, b):
         return jnp.dot(a, b, preferred_element_type=F32)
 
-    def dot_t(a, b):
-        return lax.dot_general(a, b, (((0,), (0,)), ((), ())), preferred_element_type=F32)
 
     def work_rows(k):
         return pl.ds(pl.multiple_of(k * size, size), size)
@@ -314,7 +312,7 @@
         f = step(t, l)
         rounded = (value * slope[f, k]).astype(BF16)
         scaled[f, k] = rounded
-        work[0, work_rows(k), :] = dot_t(two[l, k], rounded)
+        work[0, work_rows(k), :] = dot(two_t[l, k], rounded)
         grad[k] = value
         product = value * silu[f, k]
         gate_acc[l, k] = product if t == 0 else gate_acc[l, k] + product
@@ -354,7 +352,7 @@
                 copy_b(f, d, c, partner(d)).wait_recv()
             for b in range(per):
                 k = c * per + b
-                term = dot_t(one[l, k], ret[f, k].reshape(size, tokens))
+                term = dot(one_t[l, k], ret[f, k].reshape(size, tokens))
                 value = jnp.where(l < count, grad[k] + term, grad[k])
                 then(k, value)
                 if t == 1 and l == 0:
@@ -417,6 +415,12 @@
 
         each_block(block)
 
+    def turn_over(source, target, l):
+        def block(k):
+            target[l, k] = source[l, k].T
+
+        each_block(block)
+
     load_inp(0).wait()
     load_one(0).wait()
     start(0)
@@ -456,12 +460,15 @@
         widen(l + 1)
         load_two(l + 1).wait()
     load_arr.wait()
+    turn_over(two, two_t, top)
     forward(
         0, top, lambda k: back(0, top, k, arr[k].astype(F32)), receive(turn), send(turn)
     )
     turn += 1
     scatter_b(step(0, top))
     for l in range(top, 0, -1):
+        turn_over(one, one_t, l)
+        turn_over(two, two_t, l - 1)
         backward(0, l, functools.partial(back, 0, l - 1), receive(turn), send(turn))
         turn += 1
         scatter_b(step(0, l - 1))
@@ -469,6 +476,7 @@
     def leave(k, value):
         hop_out[k] = value.astype(BF16)
 
+    turn_over(one, one_t, 0)
     backward(0, 0, leave, receive(turn), send(turn))
     turn += 1
 
@@ -570,6 +578,8 @@
         scratch_shapes=[
             pltpu.VMEM((moments,) + block, BF16),
             pltpu.VMEM(block, BF16),
+            pltpu.VMEM(factor, BF16),
+            pltpu.VMEM(factor, BF16),
             pltpu.VMEM(factor, BF16),
             pltpu.VMEM(factor, BF16),
             pltpu.VMEM((slots, blocks, size), F32),

time: 89.9 us -> 89.6 us (level)
  no operation moved by 1% of the time
where the time goes in v5:
time: 89.6 us; the launch traced here: 89.4 us
  Pallas kernels  88.1 us (98%)
  between operations  1.29 us (1%)
    pallas_call x1, Pallas kernels, fused_shards(): pl.pallas_call(kernel, out_shape=[pltpu.VMEM(block, BF16), pltpu.VMEM(fac...  86.3 us
    pallas_call x1, Pallas kernels, store(): pl.pallas_call(store_kernel, out_shape=[jax.ShapeDtypeStruct(v.shape, v.d...  1.87 us

profile of v5, /device:TPU:0, one launch (start us, length us, event | category | flops | bytes accessed | tf_op | source)
XLA Modules:
  0.0 89.4 jit_solution(18407249755043829253)
XLA Ops:
  1.3 86.3 %shard_map.102 = (bf16[16,128,128]{2,1,0:T(8,128)(2,1)S(1)}, bf16[3,16,128,128]{3,2,1,0:T(8,128)(2,1)S(1)}, bf16[3,16,128,128]{3,2,1,0:T(8,128)(2,1)S(1)}, f32[3,16,128]{2,1,0:T(8,128)S(1)}) custom-call(bf16[2,16,128,128]{3,2,1,0:T(8,128)(2,1)} %bitcast.12, bf16[16,128,128]{2,1,0:T(8,128)(2,1)} %bitcast.13, bf16[16,128,128]{2,1,0:T(8,128)(2,1)} %bitcast.14, ...), custom_call_target="tpu_custom_call" | custom-call | tf_op jit(solution)/shard_map/pallas_call | solution.py:568
  87.6 1.9 %shard_map.103 = (bf16[16,128,128]{2,1,0:T(8,128)(2,1)}, bf16[3,16,128,128]{3,2,1,0:T(8,128)(2,1)}, bf16[3,16,128,128]{3,2,1,0:T(8,128)(2,1)}, f32[3,16,128]{2,1,0:T(8,128)}) custom-call(bf16[16,128,128]{2,1,0:T(8,128)(2,1)S(1)} %get-tuple-element.12.refs_0_, bf16[3,16,128,128]{3,2,1,0:T(8,128)(2,1)S(1)} %get-tuple-element.13.refs_1_, ...), custom_call_target="tpu_custom_call" | custom-call | tf_op jit(solution)/shard_map/pallas_call | solution.py:546

commit v6 on v5

--- a/solution.py
+++ b/solution.py
@@ -256,13 +256,13 @@
             device_id_type=MESH,
         )
 
-    def copy_b(f, d, c, source):
-        part = pl.ds(c * per, per)
+    def copy_b(f, h, d, c, source):
+        part = pl.ds(c * per, per) if h else pl.ds(0, blocks)
         return pltpu.make_async_remote_copy(
-            src_ref=send_b.at[f, d - 1, part],
-            dst_ref=ret.at[f, part, source],
+            src_ref=send_b.at[f, d - 1, part, h],
+            dst_ref=ret.at[f, part, source, h],
             send_sem=sent_b.at[f, d - 1],
-            recv_sem=recv_b.at[f, c, d - 1],
+            recv_sem=recv_b.at[f, c if h else CHUNKS, d - 1],
             device_id={"tensor": partner(d)},
             device_id_type=MESH,
         )
@@ -287,23 +287,29 @@
 
         each_chunk(chunk, low, high)
 
-    def scatter_b(f):
+    def scatter_b(f, h):
+        part = rows // 2
+        pitch = size // repeat
+
         def chunk(c):
             for d in (3, 1, 2, 0):
                 target = partner(d)
                 for j in range(per):
                     block = c * per + j
                     tile = work[
-                        0, pl.ds(target * blocks + block, rows, stride=size // repeat), :
+                        0, pl.ds(h * part * pitch + target * blocks + block, part, stride=pitch), :
                     ].astype(BF16)
                     if d:
-                        send_b[f, d - 1, block] = tile
+                        send_b[f, d - 1, block, h] = tile
                     else:
-                        ret[f, block, me] = tile
-                if d:
-                    copy_b(f, d, c, me).start()
+                        ret[f, block, me, h] = tile
+                if d and h:
+                    copy_b(f, h, d, c, me).start()
 
         each_chunk(chunk)
+        if h == 0:
+            for d in (3, 1, 2):
+                copy_b(f, h, d, 0, me).start()
 
     def permuted(f, k):
         return perm[f, pl.ds(k * repeat, repeat)].reshape(size, tokens)
@@ -348,8 +354,13 @@
         f = step(t, l)
 
         def chunk(c):
+            @pl.when(c == 0)
+            def _():
+                for d in (1, 2, 3):
+                    copy_b(f, 0, d, c, partner(d)).wait_recv()
+
             for d in (1, 2, 3):
-                copy_b(f, d, c, partner(d)).wait_recv()
+                copy_b(f, 1, d, c, partner(d)).wait_recv()
             for b in range(per):
                 k = c * per + b
                 term = dot(one_t[l, k], ret[f, k].reshape(size, tokens))
@@ -445,13 +456,24 @@
         return lambda: forward(1, l, None, low=low, high=high)
 
     def send(n):
-        if n >= len(turns):
+        if n < 0 or n >= len(turns):
             return None
         l, (low, high) = turns[n]
         return lambda: scatter_f(1, l, low, high)
 
+    def both(*calls):
+        def run():
+            for call in calls:
+                if call is not None:
+                    call()
+
+        return run
+
+    def ahead(t, l):
+        return lambda: scatter_b(step(t, l), 0)
+
     top = slots - 1
-    turn = 0
+    turn = -1
     for l in range(top):
         load_one(l + 1).wait()
         forward(0, l, None, receive(turn), send(turn))
@@ -462,22 +484,29 @@
     load_arr.wait()
     turn_over(two, two_t, top)
     forward(
-        0, top, lambda k: back(0, top, k, arr[k].astype(F32)), receive(turn), send(turn)
+        0, top, lambda k: back(0, top, k, arr[k].astype(F32)),
+        both(ahead(0, top), receive(turn)), send(turn),
     )
     turn += 1
-    scatter_b(step(0, top))
+    scatter_b(step(0, top), 1)
     for l in range(top, 0, -1):
         turn_over(one, one_t, l)
         turn_over(two, two_t, l - 1)
-        backward(0, l, functools.partial(back, 0, l - 1), receive(turn), send(turn))
+        backward(
+            0, l, functools.partial(back, 0, l - 1),
+            both(ahead(0, l - 1), receive(turn)), send(turn),
+        )
         turn += 1
-        scatter_b(step(0, l - 1))
+        scatter_b(step(0, l - 1), 1)
 
     def leave(k, value):
         hop_out[k] = value.astype(BF16)
 
     turn_over(one, one_t, 0)
     backward(0, 0, leave, receive(turn), send(turn))
+    turn += 1
+    send(turn)()
+    receive(turn)()
     turn += 1
 
     @pl.when(section == last)
@@ -493,14 +522,14 @@
             k = c * per + b
             back(1, top, k, hop_in[k].astype(F32))
 
-    beside(arrive, receive(turn), None)
-    scatter_b(step(1, top))
+    beside(arrive, both(ahead(1, top), receive(turn)), None)
+    scatter_b(step(1, top), 1)
     for l in range(top, 0, -1):
         second_grads(l)
         if l < top:
             first_grads(l + 1)
-        backward(1, l, functools.partial(back, 1, l - 1))
-        scatter_b(step(1, l - 1))
+        backward(1, l, functools.partial(back, 1, l - 1), ahead(1, l - 1))
+        scatter_b(step(1, l - 1), 1)
     second_grads(0)
     if top > 0:
         first_grads(1)
@@ -585,9 +614,9 @@
             pltpu.VMEM((slots, blocks, size), F32),
             pltpu.VMEM((moments, max(slots - 1, 1)) + block, BF16),
             pltpu.VMEM((steps, rows, tensor, blocks, tokens), BF16),
-            pltpu.VMEM((steps, blocks, tensor, rows, tokens), BF16),
+            pltpu.VMEM((steps, blocks, tensor, 2, rows // 2, tokens), BF16),
             pltpu.VMEM((steps, 3, rows, blocks, tokens), BF16),
-            pltpu.VMEM((steps, 3, blocks, rows, tokens), BF16),
+            pltpu.VMEM((steps, 3, blocks, 2, rows // 2, tokens), BF16),
             pltpu.VMEM((3, blocks * size, tokens), F32),
             pltpu.VMEM((steps,) + block, F32),
             pltpu.VMEM((steps,) + block, F32),
@@ -598,7 +627,7 @@
             pltpu.VMEM(block, BF16),
             pltpu.VMEM(block, BF16),
             pltpu.SemaphoreType.DMA((steps, CHUNKS, 3)),
-            pltpu.SemaphoreType.DMA((steps, CHUNKS, 3)),
+            pltpu.SemaphoreType.DMA((steps, CHUNKS + 1, 3)),
             pltpu.SemaphoreType.DMA((steps, 3)),
             pltpu.SemaphoreType.DMA((steps, 3)),
             pltpu.SemaphoreType.DMA((CHUNKS,)),

time: 89.6 us -> 86.5 us (0.965)
  Pallas kernels: 88.1 us -> 85.1 us
    pallas_call x1, Pallas kernels: 86.3 us -> 83.2 us  [fused_shards(): pl.pallas_call(kernel, out_shape=[pltpu.VMEM(block, BF16), pltpu.VMEM(fac...]
where the time goes in v6:
time: 86.5 us; the launch traced here: 86.4 us
  Pallas kernels  85.1 us (98%)
  between operations  1.29 us (1%)
    pallas_call x1, Pallas kernels, fused_shards(): pl.pallas_call(kernel, out_shape=[pltpu.VMEM(block, BF16), pltpu.VMEM(fac...  83.2 us
    pallas_call x1, Pallas kernels, store(): pl.pallas_call(store_kernel, out_shape=[jax.ShapeDtypeStruct(v.shape, v.d...  1.87 us

profile of v6, /device:TPU:0, one launch (start us, length us, event | category | flops | bytes accessed | tf_op | source)
XLA Modules:
  0.0 86.4 jit_solution(16508176368260007560)
XLA Ops:
  1.3 83.2 %shard_map.102 = (bf16[16,128,128]{2,1,0:T(8,128)(2,1)S(1)}, bf16[3,16,128,128]{3,2,1,0:T(8,128)(2,1)S(1)}, bf16[3,16,128,128]{3,2,1,0:T(8,128)(2,1)S(1)}, f32[3,16,128]{2,1,0:T(8,128)S(1)}) custom-call(bf16[2,16,128,128]{3,2,1,0:T(8,128)(2,1)} %bitcast.12, bf16[16,128,128]{2,1,0:T(8,128)(2,1)} %bitcast.13, bf16[16,128,128]{2,1,0:T(8,128)(2,1)} %bitcast.14, ...), custom_call_target="tpu_custom_call" | custom-call | tf_op jit(solution)/shard_map/pallas_call | solution.py:597
  84.5 1.9 %shard_map.103 = (bf16[16,128,128]{2,1,0:T(8,128)(2,1)}, bf16[3,16,128,128]{3,2,1,0:T(8,128)(2,1)}, bf16[3,16,128,128]{3,2,1,0:T(8,128)(2,1)}, f32[3,16,128]{2,1,0:T(8,128)}) custom-call(bf16[16,128,128]{2,1,0:T(8,128)(2,1)S(1)} %get-tuple-element.12.refs_0_, bf16[3,16,128,128]{3,2,1,0:T(8,128)(2,1)S(1)} %get-tuple-element.13.refs_1_, ...), custom_call_target="tpu_custom_call" | custom-call | tf_op jit(solution)/shard_map/pallas_call | solution.py:575

commit v7 on v6

--- a/solution.py
+++ b/solution.py
@@ -449,16 +449,18 @@
     halves = [(0, half), (half, CHUNKS)]
     turns = [(l, h) for l in range(slots) for h in halves]
 
+    pause = len(turns) - 2
+
     def receive(n):
-        if n <= 0 or n > len(turns):
+        if n <= 0 or n == pause + 1:
             return None
-        l, (low, high) = turns[n - 1]
+        l, (low, high) = turns[n - 1 if n <= pause else n - 2]
         return lambda: forward(1, l, None, low=low, high=high)
 
     def send(n):
-        if n < 0 or n >= len(turns):
+        if n == pause:
             return None
-        l, (low, high) = turns[n]
+        l, (low, high) = turns[n if n < pause else n - 1]
         return lambda: scatter_f(1, l, low, high)
 
     def both(*calls):
@@ -473,7 +475,7 @@
         return lambda: scatter_b(step(t, l), 0)
 
     top = slots - 1
-    turn = -1
+    turn = 0
     for l in range(top):
         load_one(l + 1).wait()
         forward(0, l, None, receive(turn), send(turn))

time: 86.5 us -> 87.2 us (level)
  no operation moved by 1% of the time
where the time goes in v7:
time: 87.2 us; the launch traced here: 87 us
  Pallas kernels  85.7 us (98%)
  between operations  1.29 us (1%)
    pallas_call x1, Pallas kernels, fused_shards(): pl.pallas_call(kernel, out_shape=[pltpu.VMEM(block, BF16), pltpu.VMEM(fac...  83.9 us
    pallas_call x1, Pallas kernels, store(): pl.pallas_call(store_kernel, out_shape=[jax.ShapeDtypeStruct(v.shape, v.d...  1.87 us

profile of v7, /device:TPU:0, one launch (start us, length us, event | category | flops | bytes accessed | tf_op | source)
XLA Modules:
  0.0 87.0 jit_solution(12907163416304560672)
XLA Ops:
  1.3 83.9 %shard_map.102 = (bf16[16,128,128]{2,1,0:T(8,128)(2,1)S(1)}, bf16[3,16,128,128]{3,2,1,0:T(8,128)(2,1)S(1)}, bf16[3,16,128,128]{3,2,1,0:T(8,128)(2,1)S(1)}, f32[3,16,128]{2,1,0:T(8,128)S(1)}) custom-call(bf16[2,16,128,128]{3,2,1,0:T(8,128)(2,1)} %bitcast.12, bf16[16,128,128]{2,1,0:T(8,128)(2,1)} %bitcast.13, bf16[16,128,128]{2,1,0:T(8,128)(2,1)} %bitcast.14, ...), custom_call_target="tpu_custom_call" | custom-call | tf_op jit(solution)/shard_map/pallas_call | solution.py:599
  85.2 1.9 %shard_map.103 = (bf16[16,128,128]{2,1,0:T(8,128)(2,1)}, bf16[3,16,128,128]{3,2,1,0:T(8,128)(2,1)}, bf16[3,16,128,128]{3,2,1,0:T(8,128)(2,1)}, f32[3,16,128]{2,1,0:T(8,128)}) custom-call(bf16[16,128,128]{2,1,0:T(8,128)(2,1)S(1)} %get-tuple-element.12.refs_0_, bf16[3,16,128,128]{3,2,1,0:T(8,128)(2,1)S(1)} %get-tuple-element.13.refs_1_, ...), custom_call_target="tpu_custom_call" | custom-call | tf_op jit(solution)/shard_map/pallas_call | solution.py:577

commit v8 on v6

--- a/solution.py
+++ b/solution.py
@@ -450,14 +450,12 @@
     turns = [(l, h) for l in range(slots) for h in halves]
 
     def receive(n):
-        if n <= 0 or n > len(turns):
+        if n <= 0:
             return None
         l, (low, high) = turns[n - 1]
         return lambda: forward(1, l, None, low=low, high=high)
 
     def send(n):
-        if n < 0 or n >= len(turns):
-            return None
         l, (low, high) = turns[n]
         return lambda: scatter_f(1, l, low, high)
 
@@ -473,7 +471,7 @@
         return lambda: scatter_b(step(t, l), 0)
 
     top = slots - 1
-    turn = -1
+    turn = 0
     for l in range(top):
         load_one(l + 1).wait()
         forward(0, l, None, receive(turn), send(turn))
@@ -504,9 +502,6 @@
 
     turn_over(one, one_t, 0)
     backward(0, 0, leave, receive(turn), send(turn))
-    turn += 1
-    send(turn)()
-    receive(turn)()
     turn += 1
 
     @pl.when(section == last)

time: 86.5 us -> 86.7 us (level)
  no operation moved by 1% of the time
where the time goes in v8:
time: 86.7 us; the launch traced here: 86.1 us
  Pallas kernels  84.8 us (98%)
  between operations  1.29 us (1%)
    pallas_call x1, Pallas kernels, fused_shards(): pl.pallas_call(kernel, out_shape=[pltpu.VMEM(block, BF16), pltpu.VMEM(fac...  82.9 us
    pallas_call x1, Pallas kernels, store(): pl.pallas_call(store_kernel, out_shape=[jax.ShapeDtypeStruct(v.shape, v.d...  1.87 us

profile of v8, /device:TPU:0, one launch (start us, length us, event | category | flops | bytes accessed | tf_op | source)
XLA Modules:
  0.0 86.1 jit_solution(12135121749885194687)
XLA Ops:
  1.3 82.9 %shard_map.102 = (bf16[16,128,128]{2,1,0:T(8,128)(2,1)S(1)}, bf16[3,16,128,128]{3,2,1,0:T(8,128)(2,1)S(1)}, bf16[3,16,128,128]{3,2,1,0:T(8,128)(2,1)S(1)}, f32[3,16,128]{2,1,0:T(8,128)S(1)}) custom-call(bf16[2,16,128,128]{3,2,1,0:T(8,128)(2,1)} %bitcast.12, bf16[16,128,128]{2,1,0:T(8,128)(2,1)} %bitcast.13, bf16[16,128,128]{2,1,0:T(8,128)(2,1)} %bitcast.14, ...), custom_call_target="tpu_custom_call" | custom-call | tf_op jit(solution)/shard_map/pallas_call | solution.py:592
  84.2 1.9 %shard_map.103 = (bf16[16,128,128]{2,1,0:T(8,128)(2,1)}, bf16[3,16,128,128]{3,2,1,0:T(8,128)(2,1)}, bf16[3,16,128,128]{3,2,1,0:T(8,128)(2,1)}, f32[3,16,128]{2,1,0:T(8,128)}) custom-call(bf16[16,128,128]{2,1,0:T(8,128)(2,1)S(1)} %get-tuple-element.12.refs_0_, bf16[3,16,128,128]{3,2,1,0:T(8,128)(2,1)S(1)} %get-tuple-element.13.refs_1_, ...), custom_call_target="tpu_custom_call" | custom-call | tf_op jit(solution)/shard_map/pallas_call | solution.py:570
